TPU v7x, 256 devices: a whole 4x4x8 slice. The times are simulated.
256 devices in a mesh: seq: 32 (over y, x, core), tp: 8 (over z).
Axes of the slice: x: 4, y: 4, z: 8, core: 2. Of those that a mesh axis runs over, the one named last changes fastest.
Arguments:
- queries: bfloat16 [8192, 8192], P('seq', 'tp'), may hold values from -5 to 5
- teacher_keys: bfloat16 [8192, 1024], P('seq', 'tp'), may hold values from -5 to 5
- teacher_values: bfloat16 [8192, 1024], P('seq', 'tp'), may hold values from -6 to 6
- student_x: bfloat16 [8192, 8192], P('seq', 'tp'), may hold values from -0.59765625 to 0.59765625
- student_b: bfloat16 [8192, 128], P('seq'), may hold values from -2.09375 to 2.09375
- student_c: bfloat16 [8192, 8192], P('seq', 'tp'), may hold values from -0.29882812 to 0.29882812
- gate_input: bfloat16 [8192, 8192], P('seq', 'tp'), may hold values from -6 to 6
- step_rates: float32 [8192, 64], P('seq', 'tp'), may hold values from 0 to 1, as said below
- skip_gain: float32 [64], P('tp'), may hold values from 0.5 to 1.5
- doc_ids: int32 [8192], P('seq'), may hold values from 0 to 7, as said below
Outputs:
- grad_x: bfloat16 [8192, 8192], P('seq', 'tp')
- grad_b: bfloat16 [8192, 128], P(('seq', 'tp'))
- grad_c: bfloat16 [8192, 8192], P('seq', 'tp')
Inputs may be any that keep to these rules, and one draw needn't show every extreme that they name: `step_rates`: positive. `doc_ids`: never falling; every document holds 1 to 4097 tokens; the one of exactly 4097 tokens begins 1 to 255 tokens after the first quarter of the 8192 tokens.
All inputs are finite; a program needn't handle non-finite values.
Results may differ from a plain program's by a relative error of at most 0.03.
Values may be sent and summed in bfloat16 or wider, within the bound.
A program may use at most 192 MiB of HBM per device.

v0:
```python
import math

import jax
import jax.numpy as jnp
from jax import lax
from jax.sharding import PartitionSpec as P

HEAD_DIM = 128
STATE = 128


def prefix(value, axis, combine, identity, reverse):
    peers, here = (lax.axis_size(axis), lax.axis_index(axis))
    everything = jax.tree.map(
        lambda part, kind: lax.all_gather(part.astype(kind), axis),
        value,
        jax.tree.map(lambda a: jnp.bfloat16 if a.dtype == jnp.float32 else a.dtype, value),
    )
    start = jax.tree.map(
        lambda part, zero: jnp.broadcast_to(jnp.asarray(zero, part.dtype), part.shape),
        value,
        identity,
    )

    def lap(k, before):
        at = peers - 1 - k if reverse else k
        reached = at > here if reverse else at < here
        new = combine(
            before, jax.tree.map(lambda part, own: part[at].astype(own.dtype), everything, value)
        )
        return jax.tree.map(lambda a, b: jnp.where(reached, a, b), new, before)

    return lax.fori_loop(0, peers, lap, start)


def contract(pattern, first_arg, second_arg):
    return jnp.einsum(pattern, first_arg, second_arg, preferred_element_type=jnp.float32)


def decay_table(block_ids, step_rates):
    log_decay = jnp.cumsum(-step_rates, axis=0)
    length = block_ids.shape[0]
    places = jnp.arange(length, dtype=jnp.int32)
    linked = (block_ids[:, None] == block_ids[None, :]) & (places[:, None] >= places[None, :])
    spread = log_decay.T[:, :, None] - log_decay.T[:, None, :]
    decays = jnp.where(linked[None], jnp.exp(jnp.where(linked[None], spread, 0.0)), 0.0)
    return (log_decay, decays)


def block_through(block_ids, log_decay):
    return jnp.where(block_ids[0] == block_ids[-1], jnp.exp(log_decay[-1]), 0.0)


def forward_combine(earlier, later):
    first_a, last_a, through_a, state_a = earlier
    first_b, last_b, through_b, state_b = later
    linked = ((last_a == first_b) | (last_a < 0) | (first_b < 0)).astype(jnp.float32)
    passing = through_b * linked
    return (
        jnp.where(first_a < 0, first_b, first_a),
        jnp.where(last_b < 0, last_a, last_b),
        through_a * passing,
        passing[:, None, None] * state_a + state_b,
    )


def reverse_combine(higher, lower):
    first_h, last_h, through_h, state_h = higher
    first_l, last_l, through_l, state_l = lower
    linked = ((last_l == first_h) | (last_l < 0) | (first_h < 0)).astype(jnp.float32)
    passing = through_l * linked
    return (
        jnp.where(first_l < 0, first_h, first_l),
        jnp.where(last_h < 0, last_l, last_h),
        through_h * passing,
        state_l + passing[:, None, None] * state_h,
    )


def chain_identity(head_count):
    missing = -jnp.ones((), jnp.int32)
    return (
        missing,
        missing,
        jnp.ones((head_count,), jnp.float32),
        jnp.zeros((head_count, STATE, HEAD_DIM), jnp.float32),
    )


def chain_element(block_ids, log_decay, student_b, x_heads):
    end_weights = jnp.where(
        (block_ids == block_ids[-1])[:, None], jnp.exp(log_decay[-1][None, :] - log_decay), 0.0
    )
    weighted = (student_b[:, None, :].astype(jnp.float32) * end_weights[:, :, None]).astype(
        jnp.bfloat16
    )
    block_state = contract("thn,thp->hnp", weighted, x_heads)
    return (block_ids[0], block_ids[-1], block_through(block_ids, log_decay), block_state)


def forward_delta(
    block_ids,
    log_decay,
    mixing,
    c_heads,
    x_heads,
    gate_heads,
    teacher,
    skip_gain,
    last_in,
    state_in,
):
    inner_part = contract("hst,thp->shp", mixing, x_heads)
    carried = jnp.where((block_ids == last_in)[:, None], jnp.exp(log_decay), 0.0)
    state_low = state_in.astype(jnp.bfloat16)
    carried_part = contract("shn,hnp->shp", c_heads, state_low) * carried[:, :, None]
    studied = inner_part + carried_part + skip_gain[None, :, None] * x_heads.astype(jnp.float32)
    opened = jax.nn.silu(gate_heads.astype(jnp.float32))
    mismatch = studied * opened - teacher.astype(jnp.float32)
    grad_y = (mismatch * opened).astype(jnp.bfloat16)
    return (carried, state_low, grad_y)


def reverse_element(block_ids, log_decay, c_heads, grad_y):
    starts = jnp.where((block_ids == block_ids[0])[:, None], jnp.exp(log_decay), 0.0)
    weighted = (c_heads.astype(jnp.float32) * starts[:, :, None]).astype(jnp.bfloat16)
    block_grad = contract("shn,shp->hnp", weighted, grad_y)
    return (block_ids[0], block_ids[-1], block_through(block_ids, log_decay), block_grad)


def backward(
    block_ids,
    log_decay,
    decays,
    mixing,
    student_b,
    c_heads,
    x_heads,
    grad_y,
    carried,
    state_low,
    skip_gain,
    first_out,
    grad_in,
):
    to_next = jnp.where(
        (block_ids == first_out)[:, None], jnp.exp(log_decay[-1][None, :] - log_decay), 0.0
    )
    grad_low = grad_in.astype(jnp.bfloat16)
    grad_x = (
        contract("hst,shp->thp", mixing, grad_y)
        + contract("tn,hnp->thp", student_b, grad_low) * to_next[:, :, None]
        + skip_gain[None, :, None] * grad_y.astype(jnp.float32)
    )
    grad_mixing = (contract("shp,thp->hst", grad_y, x_heads) * decays).astype(jnp.bfloat16)
    grad_c = (
        contract("hst,tn->shn", grad_mixing, student_b)
        + contract("shp,hnp->shn", grad_y, state_low) * carried[:, :, None]
    )
    head_terms = contract("hst,shn->tn", grad_mixing, c_heads) + jnp.sum(
        contract("thp,hnp->thn", x_heads, grad_low) * to_next[:, :, None], axis=1
    )
    return (grad_x.astype(jnp.bfloat16), grad_c.astype(jnp.bfloat16), head_terms)


def shards(
    queries,
    teacher_keys,
    teacher_values,
    student_x,
    student_b,
    student_c,
    gate_input,
    step_rates,
    skip_gain,
    doc_ids,
):
    length = queries.shape[0]
    head_count = queries.shape[1] // HEAD_DIM
    kv_count = teacher_keys.shape[1] // HEAD_DIM
    groups = head_count // kv_count
    device = lax.axis_index("seq")
    query_pos = device * length + jnp.arange(length, dtype=jnp.int32)
    grouped = queries.reshape(length, kv_count, groups, HEAD_DIM)
    score_scale = 1.0 / math.sqrt(HEAD_DIM)
    key_rows = lax.all_gather(teacher_keys, "seq", axis=0, tiled=True)
    value_rows = lax.all_gather(teacher_values, "seq", axis=0, tiled=True)
    key_ids = lax.all_gather(doc_ids, "seq", axis=0, tiled=True)
    piece_rows = key_rows.shape[0]
    key_heads = key_rows.reshape(piece_rows, kv_count, HEAD_DIM)
    value_heads = value_rows.reshape(piece_rows, kv_count, HEAD_DIM)
    key_pos = jnp.arange(piece_rows, dtype=jnp.int32)
    allowed = (
        (doc_ids[:, None] == key_ids[None, :]) & (query_pos[:, None] >= key_pos[None, :]) & True
    )
    allowed = allowed[:, None, None, :]
    scores = contract("tkgp,skp->tkgs", grouped, key_heads) * score_scale
    scores = jnp.where(allowed, scores, -1e30)
    running = jnp.full((length, kv_count, groups), -1e30, jnp.float32)
    newest = jnp.maximum(running, jnp.max(scores, axis=3))
    weights = jnp.where(allowed, jnp.exp(scores - newest[..., None]), 0.0)
    weight_sum = jnp.sum(weights, axis=3)
    weighted = contract("tkgs,skp->tkgp", weights.astype(jnp.bfloat16), value_heads)
    running, weight_sum, weighted = (newest, weight_sum, weighted)
    teacher = (
        (weighted / weight_sum[..., None])
        .astype(jnp.bfloat16)
        .reshape(length, head_count, HEAD_DIM)
    )
    x_heads = student_x.reshape(length, head_count, HEAD_DIM)
    c_heads = student_c.reshape(length, head_count, STATE)
    gate_heads = gate_input.reshape(length, head_count, HEAD_DIM)
    log_decay, decays = decay_table(doc_ids, step_rates)
    mixing = (contract("shn,tn->hst", c_heads, student_b) * decays).astype(jnp.bfloat16)
    element = chain_element(doc_ids, log_decay, student_b, x_heads)
    incoming = prefix(element, "seq", forward_combine, chain_identity(head_count), False)
    carried, state_low, grad_y = forward_delta(
        doc_ids,
        log_decay,
        mixing,
        c_heads,
        x_heads,
        gate_heads,
        teacher,
        skip_gain,
        incoming[1],
        incoming[3],
    )
    back_element = reverse_element(doc_ids, log_decay, c_heads, grad_y)
    outgoing = prefix(back_element, "seq", reverse_combine, chain_identity(head_count), True)
    grad_x, grad_c, head_terms = backward(
        doc_ids,
        log_decay,
        decays,
        mixing,
        student_b,
        c_heads,
        x_heads,
        grad_y,
        carried,
        state_low,
        skip_gain,
        outgoing[0],
        outgoing[3],
    )
    grad_b = lax.psum_scatter(
        head_terms.astype(jnp.bfloat16), "tp", scatter_dimension=0, tiled=True
    )
    return (
        grad_x.reshape(length, head_count * HEAD_DIM),
        grad_b,
        grad_c.reshape(length, head_count * STATE),
    )


def solution(mesh):
    placed = (
        P("seq", "tp"),
        P("seq", "tp"),
        P("seq", "tp"),
        P("seq", "tp"),
        P("seq", None),
        P("seq", "tp"),
        P("seq", "tp"),
        P("seq", "tp"),
        P("tp"),
        P("seq"),
    )
    return jax.shard_map(
        shards,
        mesh=mesh,
        in_specs=placed,
        out_specs=(P("seq", "tp"), P(("seq", "tp"), None), P("seq", "tp")),
        check_vma=False,
    )
```

profile of v0, /device:TPU:8, one launch (start us, length us, event | category | flops | bytes accessed | tf_op | source)
XLA Modules:
  0.0 597.2 jit_solution(11490264501580742296)
XLA Ops:
  8.0 1.6 copy.111
  11.1 1.2 copy.101
  13.4 1.3 dynamic-slice
  14.7 2.0 fusion.60
  16.8 2.0 broadcast_compare_fusion.3
  21.6 21.3 %all-gather.2 = bf16[32,1,8]{2,1,0:T(2,128)(2,1)S(1)} all-gather(bf16[1,1,8]{2,1,0:T(2,128)(2,1)S(1)} %bitcast.211), channel_id=1, replica_groups=mesh['seq'=32,'tp'=8] {'seq'}, dimensions={0}, use_global_device_ids=true | all-gather | bytes 528 | tf_op jit(solution)/shard_map/all_gather | solution.py:15
  43.0 1.2 copy.146
  44.2 2.4 copy.109
  46.6 1.4 slice_dynamic-update-slice_fusion
  48.0 14.2 %all-reduce.2 = (s32[32]{0:T(128)S(1)}, s32[32]{0:T(128)S(1)}) all-reduce(s32[32]{0:T(128)S(1)} %get-tuple-element.499, s32[32]{0:T(128)S(1)} %slice_dynamic-update-slice_fusion), channel_id=1, replica_groups=mesh['seq'=32,'tp'=8] {'seq'}, use_global_device_ids=true, to_apply=%add | all-reduce | flops 64 | bytes 512
  62.2 22.6 %all-gather.3 = s32[32,1,256]{2,1,0:T(1,128)S(1)} all-gather(s32[1,1,256]{2,1,0:T(1,128)} %bitcast.209), channel_id=1, replica_groups=mesh['seq'=32,'tp'=8] {'seq'}, dimensions={0}, use_global_device_ids=true | all-gather | bytes 33792 | tf_op jit(solution)/shard_map/all_gather | solution.py:188
  85.8 1.5 fusion.13
  87.3 1.4 convolution_bitcast_fusion.5
  88.7 3.7 fusion.9
  92.5 25.4 %fusion.2 = (f32[256,8]{0,1:T(8,128)S(1)}, f32[8192,256,8]{1,0,2:T(8,128)}) fusion(pred[256,8192]{0,1:T(8,128)(4,1)S(1)} %fusion.9, bf16[8192,128]{1,0:T(8,128)(2,1)} %all-gather.9.cloned.1.call-done, bf16[256,1024]{1,0:T(8,128)(2,1)S(1)} %copy-done), kind=kOutput, calls=%fused_computation.8 | convolution fusion | flops 4345296896 | bytes 71835648 | tf_op jit(solution)/shard_map/tkgp,skp->tkgs/dot_general | solution.py:37
  117.9 22.1 %fusion.3 = f32[256,8]{0,1:T(8,128)S(1)} fusion(f32[8192,256,8]{1,0,2:T(8,128)} %get-tuple-element.502, f32[256,8]{0,1:T(8,128)S(1)} %broadcast_maximum_fusion, pred[256,8192]{0,1:T(8,128)(4,1)S(1)} %fusion.9), kind=kLoop, calls=%fused_computation.9 | loop fusion | flops 83884032 | bytes 69222400 | tf_op jit(solution)/shard_map/reduce_sum | solution.py:202
  140.0 26.6 %divide_convert_fusion = bf16[1,128,256,8]{2,1,3,0:T(8,128)(2,1)} fusion(f32[8192,256,8]{1,0,2:T(8,128)} %get-tuple-element.502, f32[256,8]{0,1:T(8,128)S(1)} %broadcast_maximum_fusion, pred[256,8192]{0,1:T(8,128)(4,1)S(1)} %fusion.9, bf16[8192,128]{0,1:T(8,128)(2,1)} %all-gather.11.cloned.1.call-done, f32[256,8]{0,1:T(8,128)S(1)} %fusion.3), kind=kOutput, calls=%fused_computation.53 | convolution fusion | flops 4379377664 | bytes 71843840 | tf_op jit(solution)/shard_map/tkgs,skp->tkgp/dot_general | solution.py:37
  166.7 7.8 %all-gather.13.cloned.1.call-done = bf16[256,128,128]{2,1,0:T(8,128)(2,1)} async-done(((bf16[8,128,128]{2,1,0:T(8,128)(2,1)}), bf16[256,128,128]{2,1,0:T(8,128)(2,1)}) %all-gather.13.cloned.1.call-update) | async-done | bytes 8388624 | tf_op jit(solution)/shard_map/all_gather | solution.py:15
  174.4 157.6 %while.34 = (s32[]{:T(128)}, s32[]{:T(128)}, f32[8,128,128]{2,1,0:T(8,128)S(1)}, s32[]{:T(128)}, s32[32]{0:T(128)S(1)}, /*index=5*/bf16[32,8]{1,0:T(8,128)(2,1)S...) while((s32[]{:T(128)}, s32[]{:T(128)}, ...), condition=%wide.region_3.4_spmd.clone, body=%wide.region_2.3_spmd.clone.sunk | while | flops 655389 | bytes 1311030 | solution.py:33
  332.1 2.7 fusion.33
  338.3 2.0 copy.128
  340.3 2.8 convolution_bitcast_fusion.6
  343.1 50.4 %all-gather.15.cloned.1.call-done = bf16[256,128,128]{2,1,0:T(8,128)(2,1)} async-done(((bf16[8,128,128]{2,1,0:T(8,128)(2,1)}), bf16[256,128,128]{2,1,0:T(8,128)(2,1)}) %all-gather.15.cloned.1.call-update) | async-done | bytes 8388624 | tf_op jit(solution)/shard_map/all_gather | solution.py:15
  393.5 157.9 %while.35 = (s32[]{:T(128)}, s32[]{:T(128)}, f32[8,128,128]{2,1,0:T(8,128)S(1)}, s32[]{:T(128)}, s32[32]{0:T(128)S(1)}, /*index=5*/bf16[32,8,128,128]{3,2,1,0:T(...) while((s32[]{:T(128)}, s32[]{:T(128)}, ...), condition=%wide.region_7.8_spmd.clone, body=%wide.region_6.7_spmd.clone.sunk | while | flops 655393 | bytes 1311092 | solution.py:33
  395.4 1.1 fusion.80
  400.4 1.1 fusion.80
  405.3 1.1 fusion.80
  410.2 1.1 fusion.80
  415.2 1.1 fusion.80
  420.1 1.1 fusion.80
  425.0 1.1 fusion.80
  430.0 1.1 fusion.80
  434.9 1.1 fusion.80
  439.9 1.1 fusion.80
  444.8 1.1 fusion.80
  449.7 1.1 fusion.80
  454.7 1.1 fusion.80
  459.6 1.1 fusion.80
  464.5 1.1 fusion.80
  469.5 1.1 fusion.80
  474.4 1.1 fusion.80
  479.3 1.1 fusion.80
  484.3 1.1 fusion.80
  509.0 1.1 fusion.80
  533.6 1.1 fusion.80
  551.9 2.3 fusion.36
  554.2 1.6 fusion.32
  556.8 33.8 %reduce-scatter.2.cloned.1.call-done = bf16[32,128]{1,0:T(8,128)(2,1)} async-done(((bf16[256,128]{1,0:T(8,128)(2,1)}), bf16[32,128]{1,0:T(8,128)(2,1)}) %reduce-scatter.2.cloned.1.call-update) | async-done | bytes 8208 | tf_op jit(solution)/shard_map/reduce_scatter | solution.py:246
  (298 shorter events, 135.4 us)
Async XLA Ops:
  7.2 85.3 %copy-start = (bf16[256,1024]{1,0:T(8,128)(2,1)S(1)}, bf16[256,1024]{1,0:T(8,128)(2,1)}, u32[]{:S(2)}) copy-start(bf16[256,1024]{1,0:T(8,128)(2,1)} %param.14) | copy-start | bytes 1572868
  7.2 81.5 %copy-start.8 = (s32[256]{0:T(256)S(1)}, s32[256]{0:T(256)}, u32[]{:S(2)}) copy-start(s32[256]{0:T(256)} %param.23) | copy-start | bytes 3076
  7.2 85.3 %all-gather.9.cloned.1.call-start = ((), (), s32[]{:S(2)}) async-start(), calls=%async_computation.1 | async-start | bytes 2162688 | tf_op jit(solution)/shard_map/all_gather | solution.py:186
  7.9 132.1 %all-gather.11.cloned.1.call-start = ((), (), s32[]{:S(2)}) async-start(), calls=%async_computation.2 | async-start | bytes 2162688 | tf_op jit(solution)/shard_map/all_gather | solution.py:187
  9.6 164.9 %all-gather.13.cloned.1.call-start = ((), (), s32[]{:S(2)}) async-start(), calls=%async_computation.4 | async-start | bytes 8650752 | tf_op jit(solution)/shard_map/all_gather | solution.py:15
  12.3 76.3 %copy-start.1 = (bf16[256,1024]{0,1:T(8,128)(2,1)}, bf16[256,1024]{0,1:T(8,128)(2,1)S(1)}, u32[]{:S(2)}) copy-start(bf16[256,1024]{0,1:T(8,128)(2,1)S(1)} %copy.101) | copy-start | bytes 1572868
  20.1 373.4 %all-gather.15.cloned.1.call-start = ((), (), s32[]{:S(2)}) async-start(), calls=%async_computation.5 | async-start | bytes 8650752 | tf_op jit(solution)/shard_map/all_gather | solution.py:15
  44.2 44.4 %copy-start.3 = (bf16[256,1024]{0,1:T(8,128)(2,1)}, bf16[256,1024]{0,1:T(8,128)(2,1)S(1)}, u32[]{:S(2)}) copy-start(bf16[256,1024]{0,1:T(8,128)(2,1)S(1)} %copy.146) | copy-start | bytes 1572868
  87.3 1.4 copy-start.6
  140.0 192.1 %copy-start.9 = (f32[8]{0:T(128)S(1)}, f32[8]{0:T(128)}, u32[]{:S(2)}) copy-start(f32[8]{0:T(128)} %param.22) | copy-start | bytes 100
  166.7 168.1 %copy-start.4 = (bf16[256,1024]{0,1:T(8,128)(2,1)S(1)}, bf16[256,1024]{0,1:T(8,128)(2,1)}, u32[]{:S(2)}) copy-start(bf16[256,1024]{0,1:T(8,128)(2,1)} %copy-done.3) | copy-start | bytes 1572868
  166.7 169.4 %copy-start.2 = (bf16[256,1024]{0,1:T(8,128)(2,1)S(1)}, bf16[256,1024]{0,1:T(8,128)(2,1)}, u32[]{:S(2)}) copy-start(bf16[256,1024]{0,1:T(8,128)(2,1)} %copy-done.1) | copy-start | bytes 1572868
  332.0 4.8 copy-start.7
  335.8 254.8 %reduce-scatter.2.cloned.1.call-start = ((), (), s32[]{:S(2)}) async-start(), calls=%async_computation.3 | async-start | bytes 73728 | tf_op jit(solution)/shard_map/reduce_scatter | solution.py:246
  336.8 1.5 copy-start.5
Sparse Core Ops, SparseCore 0:
  10.6 51.2 all-gather.8
  64.9 49.3 all-gather.10
  116.9 57.5 all-gather.12
  335.9 57.5 all-gather.14
  554.4 36.2 reduce-scatter.1
where the time goes:
time: 602 us; the launch traced here: 597 us
  loops' own time  168 us (28%)
  other arithmetic  101 us (17%)
  waiting for transfers between devices  92.7 us (15%)
  local copies, waits for them, and re-layouts  92.4 us (15%)
  matrix products  68.8 us (11%)
  blocking collectives  58.1 us (10%)
  between operations  15.4 us (3%)
    another operation x2, loops' own time, prefix(): return lax.fori_loop(0, peers, lap, start)  168 us
    dynamic_slice x128, local copies, waits for them, and re-layouts, lap(): part[at].astype(own.dtype)  76.6 us
    select_n x64, other arithmetic, lap(): return jax.tree.map(lambda a, b: jnp.where(reached, a, b), new, before)  69.9 us
    dot_general x14, matrix products, contract(): jnp.einsum(pattern, first_arg, second_arg, preferred_element_type=jnp.flo...  68.8 us
    all_gather x2, waiting for transfers between devices, prefix(): lax.all_gather(part.astype(kind), axis)  58.2 us
    reduce_scatter x1, waiting for transfers between devices, shards(): lax.psum_scatter(head_terms.astype(jnp.bfloat16), 'tp', scatter_dimension...  33.8 us
    all_gather x1, blocking collectives, shards(): key_ids = lax.all_gather(doc_ids, 'seq', axis=0, tiled=True)  22.6 us
    reduce_sum x1, other arithmetic, shards(): weight_sum = jnp.sum(weights, axis=3)  22.1 us
  transfers between devices with their start and end apart: 5, of which 3 were waited for; matrix products, arithmetic and copies ran while one was open for 18% of the time, Pallas kernels for 0%

commit v1 on v0

v1 whole, which is shorter than its diff:
```python
import functools
import math

import jax
import jax.numpy as jnp
from jax import lax
from jax.experimental import pallas as pl
from jax.experimental.pallas import tpu as pltpu
from jax.sharding import PartitionSpec as P

MESH = pl.DeviceIdType.MESH
F32 = jnp.float32
BF16 = jnp.bfloat16

T = 256
H = 8
D = 128
FEAT = 16
KROWS = D + FEAT
FAR = 16
CHUNK = 4
PIECES = 32
PER = PIECES // H
PROWS = D // PER
META = 16
BIG = 1e30
LOG2E = math.log2(math.e)
SCALE2 = LOG2E / math.sqrt(D)


def dot(a, b):
    return lax.dot_general(a, b, (((1,), (0,)), ((), ())), preferred_element_type=F32)


def dot_t(a, b):
    return lax.dot_general(a, b, (((1,), (1,)), ((), ())), preferred_element_type=F32)


def head_lanes(h):
    return pl.ds(pl.multiple_of(h * D, D), D)


def wide(a, n):
    return jnp.concatenate([a] * n, axis=1)


def kernel(
    ids_ref,
    rates_ref,
    skip_ref,
    q_ref,
    k_ref,
    v_ref,
    x_ref,
    b_ref,
    c_ref,
    gate_ref,
    gx_ref,
    gb_ref,
    gc_ref,
    own_k,
    own_v,
    far_k,
    far_v,
    qp,
    acc,
    top,
    log_row,
    log_col,
    mask,
    mask_t,
    decay,
    decay_t,
    mix_t,
    wc_t,
    b_t,
    ids_col,
    inner,
    g_ref,
    gx_part,
    h_term,
    state_send,
    state_recv,
    entry_send,
    entry_recv,
    grad_send,
    grad_recv,
    exit_send,
    exit_recv,
    tp_send,
    tp_recv,
    kv_send_sem,
    kv_recv_sem,
    send_sem,
    recv_sem,
):
    me = lax.axis_index("seq")
    z = lax.axis_index("tp")
    n_seq, n_tp = PIECES, 8

    def clear(j, carry):
        at = pl.ds(pl.multiple_of(j * T, T), T)
        far_k[0:D, at] = jnp.zeros((D, T), BF16)
        far_k[D:KROWS, at] = jnp.full((FEAT, T), -BIG, BF16)
        far_k[KROWS:, at] = jnp.zeros((T - KROWS, T), BF16)
        far_v[at, 0:D] = jnp.zeros((T, D), BF16)
        far_v[at, D:] = jnp.ones((T, D), BF16)
        return carry

    lax.fori_loop(0, FAR, clear, 0)

    barrier = pltpu.get_barrier_semaphore()

    def greet_seq(k, carry):
        pl.semaphore_signal(
            barrier, inc=1, device_id=(lax.rem(me + k, n_seq), z), device_id_type=MESH
        )
        return carry

    def greet_tp(k, carry):
        pl.semaphore_signal(
            barrier, inc=1, device_id=(me, lax.rem(z + k, n_tp)), device_id_type=MESH
        )
        return carry

    lax.fori_loop(1, n_seq, greet_seq, 0)
    lax.fori_loop(1, n_tp, greet_tp, 0)

    ids_row = ids_ref[...].astype(F32)
    first_id = ids_row[:, 0:1]
    last_id = ids_row[:, T - 1 : T]
    feat_row = lax.broadcasted_iota(jnp.int32, (FEAT, T), 0).astype(F32)
    own_k[0:D, :] = k_ref[...].astype(F32).T.astype(BF16)
    own_k[D:KROWS, :] = jnp.where(
        feat_row == jnp.broadcast_to(ids_row, (FEAT, T)), 0.0, -BIG
    ).astype(BF16)
    own_k[KROWS:, :] = jnp.zeros((T - KROWS, T), BF16)
    own_v[:, 0:D] = v_ref[...]
    own_v[:, D:] = jnp.ones((T, D), BF16)
    b_t[...] = b_ref[...].astype(F32).T.astype(BF16)
    idc = jnp.broadcast_to(ids_row, (D, T)).T
    ids_col[...] = idc

    row = lax.broadcasted_iota(jnp.int32, (T, T), 0)
    col = lax.broadcasted_iota(jnp.int32, (T, T), 1)
    log_row[...] = -LOG2E * lax.dot_general(
        rates_ref[...],
        (row <= col).astype(F32),
        (((1,), (0,)), ((), ())),
        precision=lax.Precision.HIGHEST,
        preferred_element_type=F32,
    )
    same = wide(idc, 2) == jnp.broadcast_to(ids_row, (T, T))
    mask[...] = jnp.where(same & (row >= col), 0.0, -BIG)
    mask_t[...] = jnp.where(same & (row <= col), 0.0, -BIG)

    end_bias = jnp.where(ids_row == last_id, 0.0, -BIG)
    whole = jnp.where(first_id == last_id, 1.0, 0.0)
    meta_row = lax.broadcasted_iota(jnp.int32, (META, D), 0)

    def states(h, carry):
        lr = log_row[pl.ds(h, 1), :]
        lend = lr[:, T - 1 : T]
        weight = jnp.exp2(lend - lr + end_bias)
        wt = (b_t[...].astype(F32) * jnp.broadcast_to(weight, (D, T))).astype(BF16)
        st = dot(wt, x_ref[:, head_lanes(h)]).astype(BF16)
        thr = jnp.broadcast_to(jnp.exp2(lend) * whole, (META, D))
        high = thr.astype(BF16).astype(F32)
        meta = jnp.where(
            meta_row == 0,
            high,
            jnp.where(
                meta_row == 1,
                thr - high,
                jnp.where(
                    meta_row == 2,
                    jnp.broadcast_to(first_id, (META, D)),
                    jnp.broadcast_to(last_id, (META, D)),
                ),
            ),
        ).astype(BF16)
        for p in range(PER):
            state_send[h * PER + p, 0:PROWS, :] = st[p * PROWS : (p + 1) * PROWS, :]
            state_send[h * PER + p, PROWS:, :] = meta
        return carry

    lax.fori_loop(0, H, states, 0)

    pl.semaphore_wait(barrier, n_seq - 1 + n_tp - 1)

    def scatter(source, target, slot, peer):
        return pltpu.make_async_remote_copy(
            src_ref=source.at[peer],
            dst_ref=target.at[me],
            send_sem=send_sem.at[slot],
            recv_sem=recv_sem.at[slot],
            device_id=(peer, z),
            device_id_type=MESH,
        )

    def scatter_all(source, target, slot):
        def one(k, carry):
            scatter(source, target, slot, lax.rem(me + k, n_seq)).start()
            return carry

        lax.fori_loop(1, n_seq, one, 0)
        target[me] = source[me]

    def arrived(target, slot):
        rest = target.at[pl.ds(0, n_seq - 1)]
        pltpu.make_async_copy(rest, rest, recv_sem.at[slot]).wait()

    def left(source, slot):
        rest = source.at[pl.ds(0, n_seq - 1)]
        pltpu.make_async_copy(rest, rest, send_sem.at[slot]).wait()

    scatter_all(state_send, state_recv, 0)

    n_out = jnp.where(me < 8, 8 - me, jnp.where(me < 24, 24 - me, 31 - me))
    n_in = jnp.where(me <= 8, me, jnp.where(me <= 24, me - 8, me - 24))

    def kv_copies(d):
        at = pl.ds(pl.multiple_of(d * T, T), T)
        peer = lax.rem(me + 1 + d, n_seq)
        return (
            pltpu.make_async_remote_copy(
                src_ref=own_k.at[0:KROWS, :],
                dst_ref=far_k.at[0:KROWS, at],
                send_sem=kv_send_sem.at[0, d],
                recv_sem=kv_recv_sem.at[0, d],
                device_id=(peer, z),
                device_id_type=MESH,
            ),
            pltpu.make_async_remote_copy(
                src_ref=own_v.at[:, 0:D],
                dst_ref=far_v.at[at, 0:D],
                send_sem=kv_send_sem.at[1, d],
                recv_sem=kv_recv_sem.at[1, d],
                device_id=(peer, z),
                device_id_type=MESH,
            ),
        )

    def kv_start(d, carry):
        for copy in kv_copies(d):
            copy.start()
        return carry

    lax.fori_loop(0, n_out, kv_start, 0)

    first_bias = jnp.where(ids_row == first_id, 0.0, -BIG)
    lane = lax.broadcasted_iota(jnp.int32, (T, D), 1).astype(F32)
    q_feat = jnp.where(lane == idc, 1.0, 0.0).astype(BF16)

    def local(h, carry):
        lanes = head_lanes(h)
        lr = log_row[pl.ds(h, 1), :]
        lc = jnp.broadcast_to(lr, (D, T)).T
        log_col[h] = lc
        lrb = jnp.broadcast_to(lr, (T, T))
        lcb = wide(lc, 2)
        ch = c_ref[:, lanes]
        ct = ch.astype(F32).T
        xh = x_ref[:, lanes]
        dec = jnp.exp2(lcb - lrb + mask[...])
        decay[h] = dec
        mix = (dot(ch, b_t[...]) * dec).astype(BF16)
        inner[h] = dot(mix, xh) + skip_ref[h] * xh.astype(F32)
        dec_t = jnp.exp2(lrb - lcb + mask_t[...])
        decay_t[h] = dec_t
        mix_t[h] = (dot(b_ref[...], ct.astype(BF16)) * dec_t).astype(BF16)
        wc_t[h] = (ct * jnp.broadcast_to(jnp.exp2(lr + first_bias), (D, T))).astype(BF16)
        qh = jnp.concatenate([q_ref[:, lanes], q_feat], axis=1)
        qp[h] = qh
        s = jnp.where(row >= col, dot(qh, own_k[...]), -BIG)
        m = jnp.broadcast_to(jnp.max(s, axis=1, keepdims=True), (T, D))
        p = jnp.exp2((s - wide(m, 2)) * SCALE2)
        top[h] = m
        acc[h] = dot(p.astype(BF16), own_v[...])
        return carry

    lax.fori_loop(0, H, local, 0)

    arrived(state_recv, 0)

    def piece(c):
        got = state_recv[c]
        return got[PROWS : PROWS + 4, :].astype(F32)

    def forward(c, carry):
        total, last = carry
        got = state_recv[c].astype(F32)
        meta = got[PROWS:, :]
        entry_send[c, 0:PROWS, :] = total.astype(BF16)
        nxt = state_recv[jnp.minimum(c + 1, n_seq - 1), PROWS:, :].astype(F32)[2:3, :]
        nxt = jnp.where(c == n_seq - 1, -1.0, nxt)
        entry_send[c, PROWS:, :] = jnp.where(
            meta_row == 0,
            jnp.broadcast_to(last, (META, D)),
            jnp.broadcast_to(nxt, (META, D)),
        ).astype(BF16)
        passing = jnp.where(last == meta[2:3, :], meta[0:1, :] + meta[1:2, :], 0.0)
        return (jnp.broadcast_to(passing, (PROWS, D)) * total + got[0:PROWS, :], meta[3:4, :])

    lax.fori_loop(
        0, n_seq, forward, (jnp.zeros((PROWS, D), F32), jnp.full((1, D), -1.0, F32))
    )
    scatter_all(entry_send, entry_recv, 1)

    def attend(step):
        at = pl.ds(step * CHUNK * T, CHUNK * T)

        def head(h, carry):
            s = dot(qp[h], far_k[:, at])
            old = top[h]
            new = jnp.maximum(
                old, jnp.broadcast_to(jnp.max(s, axis=1, keepdims=True), (T, D))
            )
            p = jnp.exp2((s - wide(new, CHUNK * 2)) * SCALE2)
            shrink = jnp.exp2((old - new) * SCALE2)
            top[h] = new
            acc[h] = acc[h] * wide(shrink, 2) + dot(p.astype(BF16), far_v[at, :])
            return carry

        lax.fori_loop(0, H, head, 0)

    def kv_wait(d, carry):
        for copy in kv_copies(d):
            copy.wait_recv()
        return carry

    for step in range(FAR // CHUNK):
        lax.fori_loop(
            jnp.minimum(n_in, step * CHUNK),
            jnp.minimum(n_in, (step + 1) * CHUNK),
            kv_wait,
            0,
        )

        @pl.when(n_in > step * CHUNK)
        def _(step=step):
            attend(step)

    arrived(entry_recv, 1)
    ids_near = entry_recv[0, PROWS:, :].astype(F32)
    in_bias = jnp.where(idc == jnp.broadcast_to(ids_near[0:1, :], (T, D)), 0.0, -BIG)
    out_bias = jnp.where(idc == jnp.broadcast_to(ids_near[1:2, :], (T, D)), 0.0, -BIG)

    def state_of(ref, h):
        parts = [ref[h * PER + p, 0:PROWS, :] for p in range(PER)]
        return jnp.concatenate(parts, axis=0)

    def mismatch(h, carry):
        lanes = head_lanes(h)
        carried = jnp.exp2(log_col[h] + in_bias)
        studied = inner[h] + dot(c_ref[:, lanes], state_of(entry_recv, h)) * carried
        gate = gate_ref[:, lanes].astype(F32)
        opened = gate / (1.0 + jnp.exp(-gate))
        a = acc[h]
        teacher = (a[:, 0:D] / a[:, D:]).astype(BF16).astype(F32)
        g = ((studied * opened - teacher) * opened).astype(BF16)
        g_ref[h] = g
        bg = dot(wc_t[h], g).astype(BF16)
        for p in range(PER):
            to = h * PER + p
            grad_send[to] = bg[p * PROWS : (p + 1) * PROWS, :]

            @pl.when(to != me)
            def _():
                scatter(grad_send, grad_recv, 2, to).start()

        return carry

    lax.fori_loop(0, H, mismatch, 0)
    grad_recv[me] = grad_send[me]

    h_term[...] = jnp.zeros((T, D), F32)

    def within(h, carry):
        lanes = head_lanes(h)
        g = g_ref[h]
        xh = x_ref[:, lanes]
        gx_part[h] = dot(mix_t[h], g) + skip_ref[h] * g.astype(F32)
        gm = (dot_t(g, xh) * decay[h]).astype(BF16)
        carried = jnp.exp2(log_col[h] + in_bias)
        gc = dot(gm, b_ref[...]) + dot_t(g, state_of(entry_recv, h)) * carried
        gc_ref[:, lanes] = gc.astype(BF16)
        gm_t = (dot_t(xh, g) * decay_t[h]).astype(BF16)
        h_term[...] += dot(gm_t, c_ref[:, lanes])
        return carry

    lax.fori_loop(0, H // 2, within, 0)

    arrived(grad_recv, 2)

    def reverse(k, carry):
        total, nxt = carry
        c = n_seq - 1 - k
        meta = state_recv[c, PROWS:, :].astype(F32)
        exit_send[c] = total.astype(BF16)
        passing = jnp.where(nxt == meta[3:4, :], meta[0:1, :] + meta[1:2, :], 0.0)
        total = jnp.broadcast_to(passing, (PROWS, D)) * total + grad_recv[c].astype(F32)
        return (total, meta[2:3, :])

    lax.fori_loop(
        0, n_seq, reverse, (jnp.zeros((PROWS, D), F32), jnp.full((1, D), -1.0, F32))
    )
    scatter_all(exit_send, exit_recv, 3)

    lax.fori_loop(H // 2, H, within, 0)

    arrived(exit_recv, 3)

    def finish(h, carry):
        lanes = head_lanes(h)
        lc = log_col[h]
        to_next = jnp.exp2(jnp.broadcast_to(lc[T - 1 : T, :], (T, D)) - lc + out_bias)
        low = state_of(exit_recv, h)
        gx_ref[:, lanes] = (gx_part[h] + dot(b_ref[...], low) * to_next).astype(BF16)
        h_term[...] += dot_t(x_ref[:, lanes], low) * to_next
        return carry

    lax.fori_loop(0, H, finish, 0)

    rows = T // n_tp
    tp_send[...] = h_term[...].astype(BF16).reshape(n_tp, rows, D)

    def tp_copy(k, carry):
        peer = lax.rem(z + k, n_tp)
        pltpu.make_async_remote_copy(
            src_ref=tp_send.at[peer],
            dst_ref=tp_recv.at[z],
            send_sem=send_sem.at[4],
            recv_sem=recv_sem.at[4],
            device_id=(me, peer),
            device_id_type=MESH,
        ).start()
        return carry

    lax.fori_loop(1, n_tp, tp_copy, 0)
    tp_recv[z] = tp_send[z]
    rest = tp_recv.at[pl.ds(0, n_tp - 1)]
    pltpu.make_async_copy(rest, rest, recv_sem.at[4]).wait()
    total = jnp.zeros((rows, D), F32)
    for k in range(n_tp):
        total = total + tp_recv[k].astype(F32)
    gb_ref[...] = total.astype(BF16)

    left(state_send, 0)
    left(entry_send, 1)
    left(grad_send, 2)
    left(exit_send, 3)
    rest = tp_send.at[pl.ds(0, n_tp - 1)]
    pltpu.make_async_copy(rest, rest, send_sem.at[4]).wait()

    def kv_left(d, carry):
        for copy in kv_copies(d):
            copy.wait_send()
        return carry

    lax.fori_loop(0, n_out, kv_left, 0)


def shards(q, k, v, x, b, c, gate, rates, skip, ids):
    vmem = pl.BlockSpec(memory_space=pltpu.VMEM)
    smem = pl.BlockSpec(memory_space=pltpu.SMEM)
    return pl.pallas_call(
        kernel,
        out_shape=(
            jax.ShapeDtypeStruct((T, H * D), BF16),
            jax.ShapeDtypeStruct((T // 8, D), BF16),
            jax.ShapeDtypeStruct((T, H * D), BF16),
        ),
        in_specs=[vmem, vmem, smem] + [vmem] * 7,
        out_specs=(vmem, vmem, vmem),
        scratch_shapes=[
            pltpu.VMEM((T, T), BF16),
            pltpu.VMEM((T, T), BF16),
            pltpu.VMEM((T, FAR * T), BF16),
            pltpu.VMEM((FAR * T, T), BF16),
            pltpu.VMEM((H, T, T), BF16),
            pltpu.VMEM((H, T, T), F32),
            pltpu.VMEM((H, T, D), F32),
            pltpu.VMEM((H, T), F32),
            pltpu.VMEM((H, T, D), F32),
            pltpu.VMEM((T, T), F32),
            pltpu.VMEM((T, T), F32),
            pltpu.VMEM((H, T, T), F32),
            pltpu.VMEM((H, T, T), F32),
            pltpu.VMEM((H, T, T), BF16),
            pltpu.VMEM((H, D, T), BF16),
            pltpu.VMEM((D, T), BF16),
            pltpu.VMEM((T, D), F32),
            pltpu.VMEM((H, T, D), F32),
            pltpu.VMEM((H, T, D), BF16),
            pltpu.VMEM((H, T, D), F32),
            pltpu.VMEM((T, D), F32),
            pltpu.VMEM((PIECES, PROWS + META, D), BF16),
            pltpu.VMEM((PIECES, PROWS + META, D), BF16),
            pltpu.VMEM((PIECES, PROWS + META, D), BF16),
            pltpu.VMEM((PIECES, PROWS + META, D), BF16),
            pltpu.VMEM((PIECES, PROWS, D), BF16),
            pltpu.VMEM((PIECES, PROWS, D), BF16),
            pltpu.VMEM((PIECES, PROWS, D), BF16),
            pltpu.VMEM((PIECES, PROWS, D), BF16),
            pltpu.VMEM((8, T // 8, D), BF16),
            pltpu.VMEM((8, T // 8, D), BF16),
            pltpu.SemaphoreType.DMA((2, FAR)),
            pltpu.SemaphoreType.DMA((2, FAR)),
            pltpu.SemaphoreType.DMA((5,)),
            pltpu.SemaphoreType.DMA((5,)),
        ],
        compiler_params=pltpu.CompilerParams(
            collective_id=0, has_side_effects=True, vmem_limit_bytes=56 * 1024 * 1024
        ),
        name="distill",
    )(ids.reshape(1, T), rates.T, skip, q, k, v, x, b, c, gate)


def solution(mesh):
    placed = (
        P("seq", "tp"),
        P("seq", "tp"),
        P("seq", "tp"),
        P("seq", "tp"),
        P("seq", None),
        P("seq", "tp"),
        P("seq", "tp"),
        P("seq", "tp"),
        P("tp"),
        P("seq"),
    )
    return jax.shard_map(
        shards,
        mesh=mesh,
        in_specs=placed,
        out_specs=(P("seq", "tp"), P(("seq", "tp"), None), P("seq", "tp")),
        check_vma=False,
    )
```

time: 602 us -> 92 us (0.15)
  loops' own time: 168 us -> 0 us
  other arithmetic: 101 us -> 0 us
  waiting for transfers between devices: 92.7 us -> 0 us
  local copies, waits for them, and re-layouts: 92.4 us -> 3.33 us
  Pallas kernels: 0 us -> 86.4 us
  matrix products: 68.8 us -> 0 us
  blocking collectives: 58.1 us -> 0 us
  between operations: 15.4 us -> 0.66 us
    another operation x2 -> x0, loops' own time: 168 us -> none  [prefix(): return lax.fori_loop(0, peers, lap, start)]
    pallas_call x0 -> x1, Pallas kernels: none -> 86.4 us  [shards(): pl.pallas_call(kernel, out_shape=(jax.ShapeDtypeStruct((T, H * D), BF16),...]
    dynamic_slice x128 -> x0, local copies, waits for them, and re-layouts: 76.6 us -> none  [lap(): part[at].astype(own.dtype)]
    select_n x68 -> x0, other arithmetic: 70.2 us -> none  [the longest x64 69.9 us: lap(): return jax.tree.map(lambda a, b: jnp.where(reached, a, b), new, before)]
    dot_general x14 -> x0, matrix products: 68.8 us -> none  [contract(): jnp.einsum(pattern, first_arg, second_arg, preferred_element_type=jnp.flo...]
    all_gather x4 -> x0, waiting for transfers between devices: 58.2 us -> none  [the longest x2 58.2 us: prefix(): lax.all_gather(part.astype(kind), axis)]
    all_gather x2 -> x0, blocking collectives: 43.9 us -> none  [the longest x1 22.6 us: shards(): key_ids = lax.all_gather(doc_ids, 'seq', axis=0, tiled=True)]
    reduce_scatter x1 -> x0, waiting for transfers between devices: 33.8 us -> none  [shards(): lax.psum_scatter(head_terms.astype(jnp.bfloat16), 'tp', scatter_dimension...]
  transfers between devices with their start and end apart: 5 -> 0, of which waited for: 3 -> 0; matrix products, arithmetic and copies ran while one was open for 18% -> 0% of each run, Pallas kernels for 0% -> 0%
where the time goes in v1:
time: 92 us; the launch traced here: 90.4 us
  Pallas kernels  86.4 us (94%)
  local copies, waits for them, and re-layouts  3.33 us (4%)
    pallas_call x1, Pallas kernels, shards(): pl.pallas_call(kernel, out_shape=(jax.ShapeDtypeStruct((T, H * D), BF16),...  86.4 us
    unnamed x7, local copies, waits for them, and re-layouts  3.33 us

profile of v1, /device:TPU:8, one launch (start us, length us, event | category | flops | bytes accessed | tf_op | source)
XLA Modules:
  0.0 90.4 jit_solution(1840037205243490727)
XLA Ops:
  0.6 86.4 %distill.1 = (bf16[256,1024]{1,0:T(8,128)(2,1)}, bf16[32,128]{1,0:T(8,128)(2,1)}, bf16[256,1024]{1,0:T(8,128)(2,1)}) custom-call(s32[1,256]{1,0:T(1,128)} %bitcast.3, f32[8,256]{1,0:T(8,128)} %bitcast.2, f32[8]{0:T(128)} %skip_ref.1, bf16[256,1024]{1,0:T(8,128)(2,1)} %q_ref.1, bf16[256,128]{1,0:T(8,128)(2,1)} %k_ref.1, bf16[256,128]{1,0:T(8,128)(2,1)} %v_ref.1, ...), custom_call_target="tpu_custom_call" | custom-call | tf_op jit(solution)/shard_map/distill/pallas_call | solution.py:467
  87.0 0.0 copy-start.1
  87.0 0.0 copy-start
  87.0 1.9 %copy.16 = bf16[256,1024]{1,0:T(8,128)(2,1)} copy(bf16[256,1024]{1,0:T(8,128)(2,1)} %get-tuple-element.6) | data formatting | bytes 1048576
  89.0 0.0 copy-done.1
  89.0 0.6 copy.17
  89.6 0.0 copy-done
  89.6 0.8 copy.18
Async XLA Ops:
  87.0 1.9 %copy-start.1 = (bf16[32,128]{1,0:T(8,128)(2,1)S(1)}, bf16[32,128]{1,0:T(8,128)(2,1)}, u32[]{:S(2)}) copy-start(bf16[32,128]{1,0:T(8,128)(2,1)} %get-tuple-element.7) | copy-start | bytes 24580
  87.0 2.5 %copy-start = (bf16[256,1024]{1,0:T(8,128)(2,1)S(1)}, bf16[256,1024]{1,0:T(8,128)(2,1)}, u32[]{:S(2)}) copy-start(bf16[256,1024]{1,0:T(8,128)(2,1)} %get-tuple-element.8) | copy-start | bytes 1572868

commit v2 on v1

v2 whole, which is shorter than its diff:
```python
import functools
import math

import jax
import jax.numpy as jnp
from jax import lax
from jax.experimental import pallas as pl
from jax.experimental.pallas import tpu as pltpu
from jax.sharding import PartitionSpec as P

MESH = pl.DeviceIdType.MESH
F32 = jnp.float32
BF16 = jnp.bfloat16

T = 256
H = 8
D = 128
FEAT = 16
KROWS = D + FEAT
FAR = 16
HOPS = FAR // 2
CHUNK = 4
PIECES = 32
UNITS = 16
PER = UNITS // H
PAIR = 2
PROWS = D // PER
META = 3 * D
VMEM_LIMIT = 56 * 1024 * 1024
BIG = 1e30
LOG2E = math.log2(math.e)
SCALE2 = LOG2E / math.sqrt(D)


def dot(a, b):
    return lax.dot_general(a, b, (((1,), (0,)), ((), ())), preferred_element_type=F32)


def dot_t(a, b):
    return lax.dot_general(a, b, (((1,), (1,)), ((), ())), preferred_element_type=F32)


def head_lanes(h):
    return pl.ds(pl.multiple_of(h * D, D), D)


def wide(a, n):
    return jnp.concatenate([a] * n, axis=1)


def kernel(
    ids_ref,
    rates_ref,
    skip_ref,
    q_hbm,
    k_ref,
    v_ref,
    x_hbm,
    b_ref,
    c_hbm,
    gate_hbm,
    gx_ref,
    gb_ref,
    gc_ref,
    q_ref,
    x_ref,
    c_ref,
    gate_ref,
    own_k,
    own_v,
    far_k,
    far_v,
    qp,
    acc,
    top,
    log_row,
    log_col,
    mask,
    mask_t,
    decay,
    decay_t,
    mix_t,
    wc_t,
    b_t,
    ids_col,
    inner,
    g_ref,
    gx_part,
    h_term,
    meta,
    pass_up,
    pass_down,
    state_send,
    state_recv,
    entry_send,
    entry_recv,
    grad_send,
    grad_recv,
    exit_send,
    exit_recv,
    tp_send,
    tp_recv,
    far_send_sem,
    far_recv_sem,
    pass_send_sem,
    pass_recv_sem,
    pair_send_sem,
    pair_recv_sem,
    send_sem,
    recv_sem,
    unit_sem,
    load_sem,
):
    me = lax.axis_index("seq")
    z = lax.axis_index("tp")
    n_seq, n_tp = PIECES, 8

    base = jnp.where(me < 8, 0, jnp.where(me < 24, 8, 24))
    per = jnp.where((me >= 8) & (me < 24), 1, 2)
    count = jnp.where(per == 1, UNITS, UNITS // 2)
    base_in = jnp.where(me <= 8, 0, jnp.where(me <= 24, 8, 24))
    per_in = jnp.where((me > 8) & (me <= 24), 1, 2)

    chip = me // 2
    core = lax.rem(me, 2)
    n_out = jnp.where(chip < 4, 4 - chip, jnp.where(chip < 12, 12 - chip, 15 - chip))
    n_in = jnp.where(chip <= 4, chip, jnp.where(chip <= 12, chip - 4, chip - 12))

    low = jnp.where(chip <= 4, 0, jnp.where(chip <= 12, 8, 24))
    high = jnp.where(chip < 4, 9, jnp.where(chip < 12, 25, 31))

    barrier = pltpu.get_barrier_semaphore()

    def peer_at(k):
        return k + (k >= me).astype(jnp.int32)

    def greet_seq(k, carry):
        pl.semaphore_signal(
            barrier, inc=1, device_id=(peer_at(k), z), device_id_type=MESH
        )
        return carry

    def greet_tp(k, carry):
        pl.semaphore_signal(
            barrier, inc=1, device_id=(me, lax.rem(z + k, n_tp)), device_id_type=MESH
        )
        return carry

    lax.fori_loop(low, high, greet_seq, 0)
    lax.fori_loop(1, n_tp, greet_tp, 0)

    loads = [
        pltpu.make_async_copy(src, dst, load_sem.at[k])
        for k, (src, dst) in enumerate(
            ((x_hbm, x_ref), (c_hbm, c_ref), (q_hbm, q_ref), (gate_hbm, gate_ref))
        )
    ]
    for load in loads:
        load.start()

    ids_row = ids_ref[...].astype(F32)
    first_id = ids_row[:, 0:1]
    last_id = ids_row[:, T - 1 : T]
    feat_row = lax.broadcasted_iota(jnp.int32, (FEAT, T), 0).astype(F32)
    own_k[0:D, :] = k_ref[...].astype(F32).T.astype(BF16)
    own_k[D:KROWS, :] = jnp.where(
        feat_row == jnp.broadcast_to(ids_row, (FEAT, T)), 0.0, -BIG
    ).astype(BF16)
    own_k[KROWS:, :] = jnp.zeros((T - KROWS, T), BF16)
    own_v[:, 0:D] = v_ref[...]
    own_v[:, D:] = jnp.ones((T, D), BF16)

    pl.semaphore_wait(barrier, high - low + n_tp - 1)

    def block_copies(hop, which, src_k, src_v, peer, send_sems, recv_sems):
        at = pl.ds(pl.multiple_of((2 * hop + which) * T, T), T)
        return (
            pltpu.make_async_remote_copy(
                src_ref=src_k(at),
                dst_ref=far_k.at[0:D, at],
                send_sem=send_sems[0],
                recv_sem=recv_sems[0],
                device_id=(peer, z),
                device_id_type=MESH,
            ),
            pltpu.make_async_remote_copy(
                src_ref=src_v(at),
                dst_ref=far_v.at[at, 0:D],
                send_sem=send_sems[1],
                recv_sem=recv_sems[1],
                device_id=(peer, z),
                device_id_type=MESH,
            ),
        )

    sibling = me + 1 - 2 * core

    def own_block(at):
        return own_k.at[0:D, :]

    def own_values(at):
        return own_v.at[:, 0:D]

    def far_block(at):
        return far_k.at[0:D, at]

    def far_values(at):
        return far_v.at[at, 0:D]

    def far_copies(hop):
        peer = lax.rem(me + 2 + 2 * hop, n_seq)
        sends = (far_send_sem.at[0, hop], far_send_sem.at[1, hop])
        recvs = (far_recv_sem.at[0, hop], far_recv_sem.at[1, hop])
        return block_copies(hop, core, own_block, own_values, peer, sends, recvs)

    def pass_copies(hop, which):
        sends = (pass_send_sem.at[0, hop], pass_send_sem.at[1, hop])
        recvs = (pass_recv_sem.at[0, hop], pass_recv_sem.at[1, hop])
        return block_copies(hop, which, far_block, far_values, sibling, sends, recvs)

    def pair_copies():
        sends = (pair_send_sem.at[0], pair_send_sem.at[1])
        recvs = (pair_recv_sem.at[0], pair_recv_sem.at[1])
        return block_copies(HOPS - 1, 0, own_block, own_values, sibling, sends, recvs)

    def far_start(hop, carry):
        for copy in far_copies(hop):
            copy.start()
        return carry

    def passes(hop, which):
        return (hop < HOPS - 1) | (which == 1)

    def far_arrive(hop, carry):
        for copy in far_copies(hop):
            copy.wait_recv()

        @pl.when(passes(hop, core))
        def _():
            for copy in pass_copies(hop, core):
                copy.start()

        return carry

    def features(block, slot):
        at = pl.ds(pl.multiple_of(slot * T, T), T)
        far_k[D:KROWS, at] = jnp.where(
            feat_row == jnp.broadcast_to(meta[block][:, D:], (FEAT, T)), 0.0, -BIG
        ).astype(BF16)

    def pass_arrive(hop, carry):
        for which in range(2):
            features(jnp.maximum(me - core - 2 * hop - 2 + which, 0), 2 * hop + which)

        @pl.when(passes(hop, 1 - core))
        def _():
            for copy in pass_copies(hop, 1 - core):
                copy.wait_recv()

        return carry

    def hops(step, body):
        lax.fori_loop(
            jnp.minimum(n_in, 2 * step), jnp.minimum(n_in, 2 * step + 2), body, 0
        )

    @pl.when(core == 0)
    def _():
        for copy in pair_copies():
            copy.start()

    lax.fori_loop(0, n_out, far_start, 0)

    far_k[KROWS:, :] = jnp.zeros((T - KROWS, FAR * T), BF16)
    far_v[:, D:] = jnp.ones((FAR * T, D), BF16)

    def clear(j, carry):
        at = pl.ds(pl.multiple_of(j * T, T), T)

        @pl.when((core == 0) | (j != FAR - 2))
        def _():
            far_k[0:D, at] = jnp.zeros((D, T), BF16)
            far_k[D:KROWS, at] = jnp.full((FEAT, T), -BIG, BF16)
            far_v[at, 0:D] = jnp.zeros((T, D), BF16)

        return carry

    lax.fori_loop(2 * n_in, FAR, clear, 0)

    b_t[...] = b_ref[...].astype(F32).T.astype(BF16)
    idc = jnp.broadcast_to(ids_row, (D, T)).T
    ids_col[...] = idc

    row = lax.broadcasted_iota(jnp.int32, (T, T), 0)
    col = lax.broadcasted_iota(jnp.int32, (T, T), 1)
    log_row[...] = -LOG2E * lax.dot_general(
        rates_ref[...],
        (row <= col).astype(F32),
        (((1,), (0,)), ((), ())),
        precision=lax.Precision.HIGHEST,
        preferred_element_type=F32,
    )
    same = wide(idc, 2) == jnp.broadcast_to(ids_row, (T, T))
    mask[...] = jnp.where(same & (row >= col), 0.0, -BIG)
    mask_t[...] = jnp.where(same & (row <= col), 0.0, -BIG)

    end_bias = jnp.where(ids_row == last_id, 0.0, -BIG)
    whole = jnp.where(first_id == last_id, 1.0, 0.0)

    head_lane = lax.broadcasted_iota(jnp.int32, (H, D), 1)
    own_head = lax.broadcasted_iota(jnp.int32, (H, D), 0)
    ends = jnp.broadcast_to(jnp.exp2(log_row[:, T - 1 : T]) * whole, (H, D))
    ends = jnp.sum(jnp.where(head_lane == own_head, ends, 0.0), axis=0, keepdims=True)
    ends = jnp.where(head_lane[0:1, :] == H, first_id, ends)
    ends = jnp.where(head_lane[0:1, :] == H + 1, last_id, ends)
    meta[me] = jnp.concatenate([ends, ids_row], axis=1)

    def tell(k, carry):
        pltpu.make_async_remote_copy(
            src_ref=meta.at[me],
            dst_ref=meta.at[me],
            send_sem=send_sem.at[5],
            recv_sem=recv_sem.at[5],
            device_id=(peer_at(k), z),
            device_id_type=MESH,
        ).start()
        return carry

    def unheard(k, carry):
        @pl.when((k < low) | (k > high))
        def _():
            meta[k] = jnp.zeros((1, META), F32)

        return carry

    lax.fori_loop(low, high, tell, 0)
    lax.fori_loop(0, n_seq, unheard, 0)

    def states(h, carry):
        lr = log_row[pl.ds(h, 1), :]
        lend = lr[:, T - 1 : T]
        weight = jnp.exp2(lend - lr + end_bias)
        wt = (b_t[...].astype(F32) * jnp.broadcast_to(weight, (D, T))).astype(BF16)
        st = dot(wt, x_ref[:, head_lanes(h)]).astype(BF16)
        for p in range(PER):
            state_send[h * PER + p] = st[p * PROWS : (p + 1) * PROWS, :]
        return carry

    loads[0].wait()
    lax.fori_loop(0, H, states, 0)

    def unit_copy(source, target, phase, at, to, peer):
        return pltpu.make_async_remote_copy(
            src_ref=source.at[at],
            dst_ref=target.at[to],
            send_sem=send_sem.at[phase],
            recv_sem=unit_sem.at[phase, to],
            device_id=(peer, z),
            device_id_type=MESH,
        )

    def unit_send(source, target, phase, at, to, peer):
        @pl.when(peer != me)
        def _():
            unit_copy(source, target, phase, at, to, peer).start()

        @pl.when(peer == me)
        def _():
            target[to] = source[at]

    def unit_arrived(target, phase, to, peer):
        @pl.when(peer != me)
        def _():
            unit_copy(target, target, phase, to, to, peer).wait_recv()

    def wait_all(ref, sem, n, choices):
        for choice in choices:

            @pl.when(n == choice)
            def _(choice=choice):
                part = ref.at[pl.ds(0, choice)]
                pltpu.make_async_copy(part, part, sem).wait()

    def state_out(u, carry):
        k = jnp.where(per == 1, 0, lax.rem(u, 2))
        to = (me - base) * per + k
        unit_send(state_send, state_recv, 0, u, to, base + jnp.where(per == 1, u, u // 2))
        return carry

    lax.fori_loop(0, UNITS, state_out, 0)

    first_bias = jnp.where(ids_row == first_id, 0.0, -BIG)
    lane = lax.broadcasted_iota(jnp.int32, (T, D), 1).astype(F32)
    q_feat = jnp.where(lane == idc, 1.0, 0.0).astype(BF16)

    def local_head(h):
        lanes = head_lanes(h)
        lr = log_row[pl.ds(h, 1), :]
        lc = jnp.broadcast_to(lr, (D, T)).T
        lrb = jnp.broadcast_to(lr, (T, T))
        lcb = wide(lc, 2)
        ch = c_ref[:, lanes]
        ct = ch.astype(F32).T
        xh = x_ref[:, lanes]
        dec = jnp.exp2(lcb - lrb + mask[...])
        mix = (dot(ch, b_t[...]) * dec).astype(BF16)
        inn = dot(mix, xh) + skip_ref[h] * xh.astype(F32)
        dec_t = jnp.exp2(lrb - lcb + mask_t[...])
        mt = (dot(b_ref[...], ct.astype(BF16)) * dec_t).astype(BF16)
        wc = (ct * jnp.broadcast_to(jnp.exp2(lr + first_bias), (D, T))).astype(BF16)
        qh = jnp.concatenate([q_ref[:, lanes], q_feat], axis=1)
        s = jnp.where(row >= col, dot(qh, own_k[...]), -BIG)
        m = jnp.broadcast_to(jnp.max(s, axis=1, keepdims=True), (T, D))
        p = jnp.exp2((s - wide(m, 2)) * SCALE2)
        return lc, dec, inn, dec_t, mt, wc, qh, m, dot(p.astype(BF16), own_v[...])

    def local(i, carry):
        heads = [i * PAIR + k for k in range(PAIR)]
        done = [local_head(h) for h in heads]
        for h, (lc, dec, inn, dec_t, mt, wc, qh, m, o) in zip(heads, done):
            log_col[h] = lc
            decay[h] = dec
            inner[h] = inn
            decay_t[h] = dec_t
            mix_t[h] = mt
            wc_t[h] = wc
            rows = pl.ds(pl.multiple_of(h * T, T), T)
            qp[rows, :] = qh
            top[rows, :] = m
            acc[rows, :] = o
        return carry

    loads[1].wait()
    loads[2].wait()
    lax.fori_loop(0, H // PAIR // 2, local, 0)
    hops(0, far_arrive)
    lax.fori_loop(H // PAIR // 2, H // PAIR, local, 0)

    wait_all(meta, recv_sem.at[5], high - low, (7, 9, 17, 23, 25))
    lane_of = lax.broadcasted_iota(jnp.int32, (n_seq, D), 1)
    block_of = lax.broadcasted_iota(jnp.int32, (n_seq, D), 0)
    told = meta[...].reshape(n_seq, META)[:, 0:D]

    def lane_value(k):
        picked = jnp.sum(jnp.where(lane_of == k, told, 0.0), axis=1, keepdims=True)
        return jnp.broadcast_to(picked, (n_seq, D))

    thr = lane_value((me - base) * per // 2)
    firsts, lasts = lane_value(H), lane_value(H + 1)
    before = jnp.where(block_of == 0, -1.0, pltpu.roll(lasts, 1, 0))
    after = jnp.where(block_of == n_seq - 1, -1.0, pltpu.roll(firsts, n_seq - 1, 0))
    pass_up[...] = jnp.where(before == firsts, thr, 0.0)
    pass_down[...] = jnp.where(lasts == after, thr, 0.0)
    last_in = jnp.sum(jnp.where(block_of == me, before, 0.0), axis=0, keepdims=True)
    first_out = jnp.sum(jnp.where(block_of == me, after, 0.0), axis=0, keepdims=True)
    in_bias = jnp.where(idc == jnp.broadcast_to(last_in, (T, D)), 0.0, -BIG)
    out_bias = jnp.where(idc == jnp.broadcast_to(first_out, (T, D)), 0.0, -BIG)

    half = H * T // 2
    tile = half // 2

    def attend_rows(step, part):
        at = pl.ds(pl.multiple_of(step * CHUNK * T, CHUNK * T), CHUNK * T)
        tiles = [
            pl.ds(pl.multiple_of(part * half + k * tile, tile), tile) for k in range(2)
        ]
        scores = [dot(qp[r, :], far_k[:, at]) for r in tiles]
        weights = []
        for r, sc in zip(tiles, scores):
            old = top[r, :]
            new = jnp.maximum(
                old, jnp.broadcast_to(jnp.max(sc, axis=1, keepdims=True), (tile, D))
            )
            p = jnp.exp2((sc - wide(new, CHUNK * 2)) * SCALE2)
            weights.append((new, p.astype(BF16), jnp.exp2((old - new) * SCALE2)))
        sums = [
            acc[r, :] * wide(shrink, 2) + dot(p, far_v[at, :])
            for r, (new, p, shrink) in zip(tiles, weights)
        ]
        for r, (new, p, shrink), total in zip(tiles, weights, sums):
            top[r, :] = new
            acc[r, :] = total

    last_step = FAR // CHUNK - 1

    def attend(step, carry):
        @pl.when(n_in > 2 * step)
        def _():
            hops(step, pass_arrive)

            def rows_part(part, inner_carry):
                @pl.when(part == 1)
                def _():
                    hops(step + 1, far_arrive)

                attend_rows(step, part)
                return inner_carry

            lax.fori_loop(0, 2, rows_part, 0)

        return carry

    lax.fori_loop(0, 1, attend, 0)

    def forward(i, total):
        k = (i >= count).astype(jnp.int32)
        j = i - k * count
        slot = j * per + k
        c = base + j
        unit_arrived(state_recv, 0, slot, c)
        passing = jnp.where(j == 0, 0.0, pass_up[pl.ds(c, 1), :])
        total = jnp.broadcast_to(passing, (PROWS, D)) * total + state_recv[slot].astype(F32)
        entry_send[slot] = total.astype(BF16)

        @pl.when(c < n_seq - 1)
        def _():
            unit_send(entry_send, entry_recv, 1, slot, (me - base) * per + k, c + 1)

        return total

    lax.fori_loop(0, UNITS, forward, jnp.zeros((PROWS, D), F32))

    lax.fori_loop(1, last_step, attend, 0)

    def entry_in(u, carry):
        @pl.when(me > 0)
        def _():
            unit_arrived(entry_recv, 1, u, base_in + jnp.where(per_in == 1, u, u // 2))

        @pl.when(me == 0)
        def _():
            entry_recv[u] = jnp.zeros((PROWS, D), BF16)

        return carry

    lax.fori_loop(0, UNITS, entry_in, 0)

    def state_of(ref, h):
        parts = [ref[h * PER + p] for p in range(PER)]
        return jnp.concatenate(parts, axis=0)

    def student_head(h):
        lanes = head_lanes(h)
        carried = jnp.exp2(log_col[h] + in_bias)
        studied = inner[h] + dot(c_ref[:, lanes], state_of(entry_recv, h)) * carried
        gate = gate_ref[:, lanes].astype(F32)
        opened = gate / (1.0 + jnp.exp(-gate))
        return studied * opened * opened, opened

    def student(i, carry):
        heads = [i * PAIR + k for k in range(PAIR)]
        done = [student_head(h) for h in heads]
        for h, (ours, opened) in zip(heads, done):
            inner[h] = ours
            gx_part[h] = opened
        return carry

    loads[3].wait()
    lax.fori_loop(0, H // PAIR, student, 0)

    def mismatch_head(h):
        a = acc[pl.ds(pl.multiple_of(h * T, T), T), :]
        teacher = (a[:, 0:D] / a[:, D:]).astype(BF16).astype(F32)
        g = (inner[h] - teacher * gx_part[h]).astype(BF16)
        return g, dot(wc_t[h], g).astype(BF16)

    def mismatch(i, carry):
        heads = [i * PAIR + k for k in range(PAIR)]
        done = [mismatch_head(h) for h in heads]
        for h, (g, bg) in zip(heads, done):
            g_ref[h] = g
            for p in range(PER):
                grad_send[h * PER + p] = bg[p * PROWS : (p + 1) * PROWS, :]
        for u in [h * PER + p for h in heads for p in range(PER)]:

            @pl.when(me > 0)
            def _(u=u):
                k = jnp.where(per_in == 1, 0, lax.rem(u, 2))
                to = (me - 1 - base_in) * per_in + k
                peer = base_in + jnp.where(per_in == 1, u, u // 2)
                unit_send(grad_send, grad_recv, 2, u, to, peer)

        return carry

    @pl.when(n_in > 2 * last_step)
    def _():
        hops(last_step, pass_arrive)

    @pl.when(core == 1)
    def _():
        features(jnp.maximum(me - 1, 0), FAR - 2)
        for copy in pair_copies():
            copy.wait_recv()

    def last_part(part, carry):
        @pl.when((n_in > 2 * last_step) | (core == 1))
        def _():
            attend_rows(last_step, part)

        lax.fori_loop(part * (H // PAIR // 2), (part + 1) * (H // PAIR // 2), mismatch, 0)
        return carry

    lax.fori_loop(0, 2, last_part, 0)

    h_term[...] = jnp.zeros((T, D), F32)

    def within_head(h):
        lanes = head_lanes(h)
        g = g_ref[h]
        xh = x_ref[:, lanes]
        gx = dot(mix_t[h], g) + skip_ref[h] * g.astype(F32)
        gm = (dot_t(g, xh) * decay[h]).astype(BF16)
        carried = jnp.exp2(log_col[h] + in_bias)
        gc = dot(gm, b_ref[...]) + dot_t(g, state_of(entry_recv, h)) * carried
        gm_t = (dot_t(xh, g) * decay_t[h]).astype(BF16)
        return gx, gc.astype(BF16), dot(gm_t, c_ref[:, lanes])

    def within(i, carry):
        heads = [i * PAIR + k for k in range(PAIR)]
        done = [within_head(h) for h in heads]
        for h, (gx, gc, term) in zip(heads, done):
            gx_part[h] = gx
            gc_ref[:, head_lanes(h)] = gc
        h_term[...] += sum(term for gx, gc, term in done)
        return carry

    lax.fori_loop(0, H // PAIR // 2, within, 0)


    def reverse(i, total):
        k = (i >= count).astype(jnp.int32)
        j = count - 1 - (i - k * count)
        slot = j * per + k
        c = base + 1 + j

        @pl.when(c < n_seq)
        def _():
            unit_arrived(grad_recv, 2, slot, c)

        @pl.when(c == n_seq)
        def _():
            grad_recv[slot] = jnp.zeros((PROWS, D), BF16)

        row_of = pl.ds(jnp.minimum(c, n_seq - 1), 1)
        passing = jnp.where(j == count - 1, 0.0, pass_down[row_of, :])
        total = jnp.broadcast_to(passing, (PROWS, D)) * total + grad_recv[slot].astype(F32)
        exit_send[slot] = total.astype(BF16)
        unit_send(exit_send, exit_recv, 3, slot, (me - base) * per + k, base + j)
        return total

    lax.fori_loop(0, UNITS, reverse, jnp.zeros((PROWS, D), F32))

    lax.fori_loop(H // PAIR // 2, H // PAIR, within, 0)

    def exit_in(u, carry):
        unit_arrived(exit_recv, 3, u, base + jnp.where(per == 1, u, u // 2))
        return carry

    lax.fori_loop(0, UNITS, exit_in, 0)

    def next_decay(h):
        lc = log_col[h]
        return jnp.exp2(jnp.broadcast_to(lc[T - 1 : T, :], (T, D)) - lc + out_bias)

    def terms(i, carry):
        heads = [i * PAIR + k for k in range(PAIR)]
        h_term[...] += sum(
            dot_t(x_ref[:, head_lanes(h)], state_of(exit_recv, h)) * next_decay(h)
            for h in heads
        )
        return carry

    def finish(i, carry):
        heads = [i * PAIR + k for k in range(PAIR)]
        done = [
            (gx_part[h] + dot(b_ref[...], state_of(exit_recv, h)) * next_decay(h)).astype(BF16)
            for h in heads
        ]
        for h, gx in zip(heads, done):
            gx_ref[:, head_lanes(h)] = gx
        return carry

    lax.fori_loop(0, H // PAIR, terms, 0)

    rows = T // n_tp
    tp_send[...] = h_term[...].astype(BF16).reshape(n_tp, rows, D)

    def tp_copy(k, carry):
        peer = lax.rem(z + k, n_tp)
        pltpu.make_async_remote_copy(
            src_ref=tp_send.at[peer],
            dst_ref=tp_recv.at[z],
            send_sem=send_sem.at[4],
            recv_sem=recv_sem.at[4],
            device_id=(me, peer),
            device_id_type=MESH,
        ).start()
        return carry

    lax.fori_loop(1, n_tp, tp_copy, 0)
    tp_recv[z] = tp_send[z]
    lax.fori_loop(0, H // PAIR, finish, 0)
    rest = tp_recv.at[pl.ds(0, n_tp - 1)]
    pltpu.make_async_copy(rest, rest, recv_sem.at[4]).wait()
    total = jnp.zeros((rows, D), F32)
    for k in range(n_tp):
        total = total + tp_recv[k].astype(F32)
    gb_ref[...] = total.astype(BF16)

    first_of = (me == base).astype(jnp.int32)
    last_chain = (base == 24).astype(jnp.int32)
    no_worker = ((me == 8) | (me == 24)).astype(jnp.int32)
    sizes = (12, 14, 15, 16)
    wait_all(state_send, send_sem.at[0], UNITS - per, sizes)
    wait_all(entry_send, send_sem.at[1], UNITS - per * (1 - first_of + last_chain), sizes)
    wait_all(
        grad_send,
        send_sem.at[2],
        jnp.where(me == 0, 0, UNITS - per_in * (1 - no_worker)),
        sizes,
    )
    wait_all(exit_send, send_sem.at[3], UNITS - per, sizes)
    wait_all(meta, send_sem.at[5], high - low, (7, 9, 17, 23, 25))
    rest = tp_send.at[pl.ds(0, n_tp - 1)]
    pltpu.make_async_copy(rest, rest, send_sem.at[4]).wait()

    def far_left(hop, carry):
        for copy in far_copies(hop):
            copy.wait_send()
        return carry

    def pass_left(hop, carry):
        @pl.when(passes(hop, core))
        def _():
            for copy in pass_copies(hop, core):
                copy.wait_send()

        return carry

    lax.fori_loop(0, n_out, far_left, 0)
    lax.fori_loop(0, n_in, pass_left, 0)

    @pl.when(core == 0)
    def _():
        for copy in pair_copies():
            copy.wait_send()


def hand_over(gx_in, gb_in, gc_in, gx_out, gb_out, gc_out, gx, gb, gc, sem):
    ins = ((gx_in, gx), (gb_in, gb), (gc_in, gc))
    outs = ((gx, gx_out), (gb, gb_out), (gc, gc_out))
    get = [pltpu.make_async_copy(a, b, sem.at[k]) for k, (a, b) in enumerate(ins)]
    put = [pltpu.make_async_copy(a, b, sem.at[k]) for k, (a, b) in enumerate(outs)]
    for copy in get:
        copy.start()
    for first, second in zip(get, put):
        first.wait()
        second.start()
    for copy in put:
        copy.wait()


def shards(q, k, v, x, b, c, gate, rates, skip, ids):
    vmem = pl.BlockSpec(memory_space=pltpu.VMEM)
    smem = pl.BlockSpec(memory_space=pltpu.SMEM)
    anywhere = pl.BlockSpec(memory_space=pl.ANY)
    results = pl.pallas_call(
        kernel,
        out_shape=(
            jax.ShapeDtypeStruct((T, H * D), BF16),
            jax.ShapeDtypeStruct((T // 8, D), BF16),
            jax.ShapeDtypeStruct((T, H * D), BF16),
        ),
        in_specs=[vmem, vmem, smem, anywhere, vmem, vmem, anywhere, vmem, anywhere, anywhere],
        out_specs=(vmem, vmem, vmem),
        scratch_shapes=[
            pltpu.VMEM((T, H * D), BF16),
            pltpu.VMEM((T, H * D), BF16),
            pltpu.VMEM((T, H * D), BF16),
            pltpu.VMEM((T, H * D), BF16),
            pltpu.VMEM((T, T), BF16),
            pltpu.VMEM((T, T), BF16),
            pltpu.VMEM((T, FAR * T), BF16),
            pltpu.VMEM((FAR * T, T), BF16),
            pltpu.VMEM((H * T, T), BF16),
            pltpu.VMEM((H * T, T), F32),
            pltpu.VMEM((H * T, D), F32),
            pltpu.VMEM((H, T), F32),
            pltpu.VMEM((H, T, D), F32),
            pltpu.VMEM((T, T), F32),
            pltpu.VMEM((T, T), F32),
            pltpu.VMEM((H, T, T), F32),
            pltpu.VMEM((H, T, T), F32),
            pltpu.VMEM((H, T, T), BF16),
            pltpu.VMEM((H, D, T), BF16),
            pltpu.VMEM((D, T), BF16),
            pltpu.VMEM((T, D), F32),
            pltpu.VMEM((H, T, D), F32),
            pltpu.VMEM((H, T, D), BF16),
            pltpu.VMEM((H, T, D), F32),
            pltpu.VMEM((T, D), F32),
            pltpu.VMEM((PIECES, 1, META), F32),
            pltpu.VMEM((PIECES, D), F32),
            pltpu.VMEM((PIECES, D), F32),
            pltpu.VMEM((UNITS, PROWS, D), BF16),
            pltpu.VMEM((UNITS, PROWS, D), BF16),
            pltpu.VMEM((UNITS, PROWS, D), BF16),
            pltpu.VMEM((UNITS, PROWS, D), BF16),
            pltpu.VMEM((UNITS, PROWS, D), BF16),
            pltpu.VMEM((UNITS, PROWS, D), BF16),
            pltpu.VMEM((UNITS, PROWS, D), BF16),
            pltpu.VMEM((UNITS, PROWS, D), BF16),
            pltpu.VMEM((8, T // 8, D), BF16),
            pltpu.VMEM((8, T // 8, D), BF16),
            pltpu.SemaphoreType.DMA((2, HOPS)),
            pltpu.SemaphoreType.DMA((2, HOPS)),
            pltpu.SemaphoreType.DMA((2, HOPS)),
            pltpu.SemaphoreType.DMA((2, HOPS)),
            pltpu.SemaphoreType.DMA((2,)),
            pltpu.SemaphoreType.DMA((2,)),
            pltpu.SemaphoreType.DMA((6,)),
            pltpu.SemaphoreType.DMA((6,)),
            pltpu.SemaphoreType.DMA((4, UNITS)),
            pltpu.SemaphoreType.DMA((4,)),
        ],
        compiler_params=pltpu.CompilerParams(
            collective_id=0, has_side_effects=True, vmem_limit_bytes=VMEM_LIMIT
        ),
        name="distill",
    )(ids.reshape(1, T), rates.T, skip, q, k, v, x, b, c, gate)
    return pl.pallas_call(
        hand_over,
        out_shape=[jax.ShapeDtypeStruct(a.shape, a.dtype) for a in results],
        in_specs=[anywhere] * 3,
        out_specs=[anywhere] * 3,
        scratch_shapes=[pltpu.VMEM(a.shape, a.dtype) for a in results]
        + [pltpu.SemaphoreType.DMA((3,))],
        compiler_params=pltpu.CompilerParams(vmem_limit_bytes=60 * 1024 * 1024),
        name="hand_over",
    )(*results)


def solution(mesh):
    placed = (
        P("seq", "tp"),
        P("seq", "tp"),
        P("seq", "tp"),
        P("seq", "tp"),
        P("seq", None),
        P("seq", "tp"),
        P("seq", "tp"),
        P("seq", "tp"),
        P("tp"),
        P("seq"),
    )
    return jax.shard_map(
        shards,
        mesh=mesh,
        in_specs=placed,
        out_specs=(P("seq", "tp"), P(("seq", "tp"), None), P("seq", "tp")),
        check_vma=False,
    )
```

time: 92 us -> 64.5 us (0.70); the launches traced: 90.4 us -> 64.3 us
  Pallas kernels: 86.4 us -> 63.7 us
  local copies, waits for them, and re-layouts: 3.33 us -> 0 us
    pallas_call x1, Pallas kernels: 86.4 us -> 61.7 us  [shards(): pl.pallas_call(kernel, out_shape=(jax.ShapeDtypeStruct((T, H * D), BF16),...]
    unnamed x7 -> x0, local copies, waits for them, and re-layouts: 3.33 us -> none
    pallas_call x0 -> x1, Pallas kernels: none -> 2.04 us  [shards(): pl.pallas_call(hand_over, out_shape=[jax.ShapeDtypeStruct(a.shape, a.dtyp...]
where the time goes in v2:
time: 64.5 us; the launch traced here: 64.3 us
  Pallas kernels  63.7 us (99%)
    pallas_call x1, Pallas kernels, shards(): pl.pallas_call(kernel, out_shape=(jax.ShapeDtypeStruct((T, H * D), BF16),...  61.7 us
    pallas_call x1, Pallas kernels, shards(): pl.pallas_call(hand_over, out_shape=[jax.ShapeDtypeStruct(a.shape, a.dtyp...  2.04 us

profile of v2, /device:TPU:8, one launch (start us, length us, event | category | flops | bytes accessed | tf_op | source)
XLA Modules:
  0.0 64.3 jit_solution(7646403023752800141)
XLA Ops:
  0.6 61.7 %distill.1 = (bf16[256,1024]{1,0:T(8,128)(2,1)}, bf16[32,128]{1,0:T(8,128)(2,1)}, bf16[256,1024]{1,0:T(8,128)(2,1)}) custom-call(s32[1,256]{1,0:T(1,128)} %bitcast.3, f32[8,256]{1,0:T(8,128)} %bitcast.2, f32[8]{0:T(128)} %skip_ref.1, bf16[256,1024]{1,0:T(8,128)(2,1)} %q_hbm.1, bf16[256,128]{1,0:T(8,128)(2,1)} %k_ref.1, bf16[256,128]{1,0:T(8,128)(2,1)} %v_ref.1, ...), custom_call_target="tpu_custom_call" | custom-call | tf_op jit(solution)/shard_map/distill/pallas_call | solution.py:767
  62.3 2.0 %hand_over.1 = (bf16[256,1024]{1,0:T(8,128)(2,1)}, bf16[32,128]{1,0:T(8,128)(2,1)}, bf16[256,1024]{1,0:T(8,128)(2,1)}) custom-call(bf16[256,1024]{1,0:T(8,128)(2,1)} %get-tuple-element.6.gx_in, bf16[32,128]{1,0:T(8,128)(2,1)} %get-tuple-element.7.gb_in, bf16[256,1024]{1,0:T(8,128)(2,1)} %get-tuple-element.8.gc_in), custom_call_target="tpu_custom_call" | custom-call | tf_op jit(solution)/shard_map/hand_over/pallas_call | solution.py:831

commit v3 on v2

--- a/solution.py
+++ b/solution.py
@@ -19,11 +19,12 @@
 KROWS = D + FEAT
 FAR = 16
 HOPS = FAR // 2
+BELOW = 3
 CHUNK = 4
 PIECES = 32
 UNITS = 16
 PER = UNITS // H
-PAIR = 2
+PAIR = 4
 PROWS = D // PER
 META = 3 * D
 VMEM_LIMIT = 56 * 1024 * 1024
@@ -106,6 +107,7 @@
     pass_recv_sem,
     pair_send_sem,
     pair_recv_sem,
+    relay_send_sem,
     send_sem,
     recv_sem,
     unit_sem,
@@ -223,15 +225,43 @@
         recvs = (pair_recv_sem.at[0], pair_recv_sem.at[1])
         return block_copies(HOPS - 1, 0, own_block, own_values, sibling, sends, recvs)
 
+    upper = (chip >= 4) & (chip < 8)
+    lower = (chip >= 8) & (chip < 12)
+    left_half = lax.rem(chip, 4) < 2
+    across = jnp.where(left_half, BELOW + 2, BELOW - 2)
+
+    def relay_copies():
+        at = pl.ds(pl.multiple_of((2 * BELOW + core) * T, T), T)
+        to = pl.ds(pl.multiple_of((2 * across + core) * T, T), T)
+        peer = jnp.where(lower, me + 2 * (across - BELOW), sibling)
+        pairs = (
+            (far_k.at[0:D, at], far_k.at[0:D, to]),
+            (far_v.at[at, 0:D], far_v.at[to, 0:D]),
+        )
+        return [
+            pltpu.make_async_remote_copy(
+                src_ref=src,
+                dst_ref=dst,
+                send_sem=relay_send_sem.at[k],
+                recv_sem=far_recv_sem.at[k, across],
+                device_id=(peer, z),
+                device_id_type=MESH,
+            )
+            for k, (src, dst) in enumerate(pairs)
+        ]
+
     def far_start(hop, carry):
-        for copy in far_copies(hop):
-            copy.start()
+        @pl.when(jnp.logical_not(upper & ((hop == across) | (hop == BELOW))))
+        def _():
+            for copy in far_copies(hop):
+                copy.start()
+
         return carry
 
     def passes(hop, which):
         return (hop < HOPS - 1) | (which == 1)
 
-    def far_arrive(hop, carry):
+    def far_take(hop):
         for copy in far_copies(hop):
             copy.wait_recv()
 
@@ -239,6 +269,11 @@
         def _():
             for copy in pass_copies(hop, core):
                 copy.start()
+
+    def far_arrive(hop, carry):
+        @pl.when(jnp.logical_not(lower & (hop == BELOW)))
+        def _():
+            far_take(hop)
 
         return carry
 
@@ -267,6 +302,11 @@
     @pl.when(core == 0)
     def _():
         for copy in pair_copies():
+            copy.start()
+
+    @pl.when(upper)
+    def _():
+        for copy in far_copies(BELOW):
             copy.start()
 
     lax.fori_loop(0, n_out, far_start, 0)
@@ -433,6 +473,12 @@
     loads[1].wait()
     loads[2].wait()
     lax.fori_loop(0, H // PAIR // 2, local, 0)
+    @pl.when(lower)
+    def _():
+        far_take(BELOW)
+        for copy in relay_copies():
+            copy.start()
+
     hops(0, far_arrive)
     lax.fori_loop(H // PAIR // 2, H // PAIR, local, 0)
 
@@ -725,8 +771,11 @@
     pltpu.make_async_copy(rest, rest, send_sem.at[4]).wait()
 
     def far_left(hop, carry):
-        for copy in far_copies(hop):
-            copy.wait_send()
+        @pl.when(jnp.logical_not(upper & (hop == across)))
+        def _():
+            for copy in far_copies(hop):
+                copy.wait_send()
+
         return carry
 
     def pass_left(hop, carry):
@@ -738,6 +787,12 @@
         return carry
 
     lax.fori_loop(0, n_out, far_left, 0)
+
+    @pl.when(lower)
+    def _():
+        for copy in relay_copies():
+            copy.wait_send()
+
     lax.fori_loop(0, n_in, pass_left, 0)
 
     @pl.when(core == 0)
@@ -818,6 +873,7 @@
             pltpu.SemaphoreType.DMA((2, HOPS)),
             pltpu.SemaphoreType.DMA((2,)),
             pltpu.SemaphoreType.DMA((2,)),
+            pltpu.SemaphoreType.DMA((2,)),
             pltpu.SemaphoreType.DMA((6,)),
             pltpu.SemaphoreType.DMA((6,)),
             pltpu.SemaphoreType.DMA((4, UNITS)),

time: 64.5 us -> 60.2 us (0.933)
  Pallas kernels: 63.7 us -> 59.4 us
    pallas_call x1, Pallas kernels: 61.7 us -> 57.4 us  [shards(): pl.pallas_call(kernel, out_shape=(jax.ShapeDtypeStruct((T, H * D), BF16),...]
where the time goes in v3:
time: 60.2 us; the launch traced here: 60.1 us
  Pallas kernels  59.4 us (99%)
  between operations  0.64 us (1%)
    pallas_call x1, Pallas kernels, shards(): pl.pallas_call(kernel, out_shape=(jax.ShapeDtypeStruct((T, H * D), BF16),...  57.4 us
    pallas_call x1, Pallas kernels, shards(): pl.pallas_call(hand_over, out_shape=[jax.ShapeDtypeStruct(a.shape, a.dtyp...  2.04 us

profile of v3, /device:TPU:8, one launch (start us, length us, event | category | flops | bytes accessed | tf_op | source)
XLA Modules:
  0.0 60.1 jit_solution(15245387904205784041)
XLA Ops:
  0.6 57.4 %distill.1 = (bf16[256,1024]{1,0:T(8,128)(2,1)}, bf16[32,128]{1,0:T(8,128)(2,1)}, bf16[256,1024]{1,0:T(8,128)(2,1)}) custom-call(s32[1,256]{1,0:T(1,128)} %bitcast.3, f32[8,256]{1,0:T(8,128)} %bitcast.2, f32[8]{0:T(128)} %skip_ref.1, bf16[256,1024]{1,0:T(8,128)(2,1)} %q_hbm.1, bf16[256,128]{1,0:T(8,128)(2,1)} %k_ref.1, bf16[256,128]{1,0:T(8,128)(2,1)} %v_ref.1, ...), custom_call_target="tpu_custom_call" | custom-call | tf_op jit(solution)/shard_map/distill/pallas_call | solution.py:822
  58.0 2.0 %hand_over.1 = (bf16[256,1024]{1,0:T(8,128)(2,1)}, bf16[32,128]{1,0:T(8,128)(2,1)}, bf16[256,1024]{1,0:T(8,128)(2,1)}) custom-call(bf16[256,1024]{1,0:T(8,128)(2,1)} %get-tuple-element.6.gx_in, bf16[32,128]{1,0:T(8,128)(2,1)} %get-tuple-element.7.gb_in, bf16[256,1024]{1,0:T(8,128)(2,1)} %get-tuple-element.8.gc_in), custom_call_target="tpu_custom_call" | custom-call | tf_op jit(solution)/shard_map/hand_over/pallas_call | solution.py:887

commit v4 on v3

--- a/solution.py
+++ b/solution.py
@@ -60,8 +60,10 @@
     b_ref,
     c_hbm,
     gate_hbm,
+    gx_hbm,
+    gb_ref,
+    gc_hbm,
     gx_ref,
-    gb_ref,
     gc_ref,
     q_ref,
     x_ref,
@@ -112,6 +114,7 @@
     recv_sem,
     unit_sem,
     load_sem,
+    store_sem,
 ):
     me = lax.axis_index("seq")
     z = lax.axis_index("tp")
@@ -697,6 +700,8 @@
     lax.fori_loop(0, UNITS, reverse, jnp.zeros((PROWS, D), F32))
 
     lax.fori_loop(H // PAIR // 2, H // PAIR, within, 0)
+    store_c = pltpu.make_async_copy(gc_ref, gc_hbm, store_sem.at[0])
+    store_c.start()
 
     def exit_in(u, carry):
         unit_arrived(exit_recv, 3, u, base + jnp.where(per == 1, u, u // 2))
@@ -746,12 +751,16 @@
     lax.fori_loop(1, n_tp, tp_copy, 0)
     tp_recv[z] = tp_send[z]
     lax.fori_loop(0, H // PAIR, finish, 0)
+    store_x = pltpu.make_async_copy(gx_ref, gx_hbm, store_sem.at[1])
+    store_x.start()
     rest = tp_recv.at[pl.ds(0, n_tp - 1)]
     pltpu.make_async_copy(rest, rest, recv_sem.at[4]).wait()
     total = jnp.zeros((rows, D), F32)
     for k in range(n_tp):
         total = total + tp_recv[k].astype(F32)
     gb_ref[...] = total.astype(BF16)
+    store_c.wait()
+    store_x.wait()
 
     first_of = (me == base).astype(jnp.int32)
     last_chain = (base == 24).astype(jnp.int32)
@@ -827,8 +836,10 @@
             jax.ShapeDtypeStruct((T, H * D), BF16),
         ),
         in_specs=[vmem, vmem, smem, anywhere, vmem, vmem, anywhere, vmem, anywhere, anywhere],
-        out_specs=(vmem, vmem, vmem),
+        out_specs=(anywhere, vmem, anywhere),
         scratch_shapes=[
+            pltpu.VMEM((T, H * D), BF16),
+            pltpu.VMEM((T, H * D), BF16),
             pltpu.VMEM((T, H * D), BF16),
             pltpu.VMEM((T, H * D), BF16),
             pltpu.VMEM((T, H * D), BF16),
@@ -878,6 +889,7 @@
             pltpu.SemaphoreType.DMA((6,)),
             pltpu.SemaphoreType.DMA((4, UNITS)),
             pltpu.SemaphoreType.DMA((4,)),
+            pltpu.SemaphoreType.DMA((2,)),
         ],
         compiler_params=pltpu.CompilerParams(
             collective_id=0, has_side_effects=True, vmem_limit_bytes=VMEM_LIMIT

time: 60.2 us -> 59.9 us (level)
  no operation moved by 1% of the time
where the time goes in v4:
time: 59.9 us; the launch traced here: 59.7 us
  Pallas kernels  59.1 us (99%)
  between operations  0.64 us (1%)
    pallas_call x1, Pallas kernels, shards(): pl.pallas_call(kernel, out_shape=(jax.ShapeDtypeStruct((T, H * D), BF16),...  57 us
    pallas_call x1, Pallas kernels, shards(): pl.pallas_call(hand_over, out_shape=[jax.ShapeDtypeStruct(a.shape, a.dtyp...  2.04 us

profile of v4, /device:TPU:8, one launch (start us, length us, event | category | flops | bytes accessed | tf_op | source)
XLA Modules:
  0.0 59.7 jit_solution(4377554984723389896)
XLA Ops:
  0.6 57.0 %distill.1 = (bf16[256,1024]{1,0:T(8,128)(2,1)}, bf16[32,128]{1,0:T(8,128)(2,1)}, bf16[256,1024]{1,0:T(8,128)(2,1)}) custom-call(s32[1,256]{1,0:T(1,128)} %bitcast.3, f32[8,256]{1,0:T(8,128)} %bitcast.2, f32[8]{0:T(128)} %skip_ref.1, bf16[256,1024]{1,0:T(8,128)(2,1)} %q_hbm.1, bf16[256,128]{1,0:T(8,128)(2,1)} %k_ref.1, bf16[256,128]{1,0:T(8,128)(2,1)} %v_ref.1, ...), custom_call_target="tpu_custom_call" | custom-call | tf_op jit(solution)/shard_map/distill/pallas_call | solution.py:831
  57.7 2.0 %hand_over.1 = (bf16[256,1024]{1,0:T(8,128)(2,1)}, bf16[32,128]{1,0:T(8,128)(2,1)}, bf16[256,1024]{1,0:T(8,128)(2,1)}) custom-call(bf16[256,1024]{1,0:T(8,128)(2,1)} %get-tuple-element.6.gx_in, bf16[32,128]{1,0:T(8,128)(2,1)} %get-tuple-element.7.gb_in, bf16[256,1024]{1,0:T(8,128)(2,1)} %get-tuple-element.8.gc_in), custom_call_target="tpu_custom_call" | custom-call | tf_op jit(solution)/shard_map/hand_over/pallas_call | solution.py:899

commit v5 on v4

--- a/solution.py
+++ b/solution.py
@@ -140,9 +140,8 @@
         return k + (k >= me).astype(jnp.int32)
 
     def greet_seq(k, carry):
-        pl.semaphore_signal(
-            barrier, inc=1, device_id=(peer_at(k), z), device_id_type=MESH
-        )
+        peer = peer_at(jnp.where(chip == 4, low + high - 1 - k, k))
+        pl.semaphore_signal(barrier, inc=1, device_id=(peer, z), device_id_type=MESH)
         return carry
 
     def greet_tp(k, carry):
@@ -302,17 +301,17 @@
             jnp.minimum(n_in, 2 * step), jnp.minimum(n_in, 2 * step + 2), body, 0
         )
 
+    @pl.when(upper)
+    def _():
+        for copy in far_copies(BELOW):
+            copy.start()
+
+    lax.fori_loop(0, n_out, far_start, 0)
+
     @pl.when(core == 0)
     def _():
         for copy in pair_copies():
             copy.start()
-
-    @pl.when(upper)
-    def _():
-        for copy in far_copies(BELOW):
-            copy.start()
-
-    lax.fori_loop(0, n_out, far_start, 0)
 
     far_k[KROWS:, :] = jnp.zeros((T - KROWS, FAR * T), BF16)
     far_v[:, D:] = jnp.ones((FAR * T, D), BF16)

time: 59.9 us -> 59.9 us (level)
  no operation moved by 1% of the time
where the time goes in v5:
time: 59.9 us; the launch traced here: 59.7 us
  Pallas kernels  59.1 us (99%)
  between operations  0.64 us (1%)
    pallas_call x1, Pallas kernels, shards(): pl.pallas_call(kernel, out_shape=(jax.ShapeDtypeStruct((T, H * D), BF16),...  57 us
    pallas_call x1, Pallas kernels, shards(): pl.pallas_call(hand_over, out_shape=[jax.ShapeDtypeStruct(a.shape, a.dtyp...  2.04 us

profile of v5, /device:TPU:8, one launch (start us, length us, event | category | flops | bytes accessed | tf_op | source)
XLA Modules:
  0.0 59.7 jit_solution(14423210624328114730)
XLA Ops:
  0.6 57.0 %distill.1 = (bf16[256,1024]{1,0:T(8,128)(2,1)}, bf16[32,128]{1,0:T(8,128)(2,1)}, bf16[256,1024]{1,0:T(8,128)(2,1)}) custom-call(s32[1,256]{1,0:T(1,128)} %bitcast.3, f32[8,256]{1,0:T(8,128)} %bitcast.2, f32[8]{0:T(128)} %skip_ref.1, bf16[256,1024]{1,0:T(8,128)(2,1)} %q_hbm.1, bf16[256,128]{1,0:T(8,128)(2,1)} %k_ref.1, bf16[256,128]{1,0:T(8,128)(2,1)} %v_ref.1, ...), custom_call_target="tpu_custom_call" | custom-call | tf_op jit(solution)/shard_map/distill/pallas_call | solution.py:830
  57.7 2.0 %hand_over.1 = (bf16[256,1024]{1,0:T(8,128)(2,1)}, bf16[32,128]{1,0:T(8,128)(2,1)}, bf16[256,1024]{1,0:T(8,128)(2,1)}) custom-call(bf16[256,1024]{1,0:T(8,128)(2,1)} %get-tuple-element.6.gx_in, bf16[32,128]{1,0:T(8,128)(2,1)} %get-tuple-element.7.gb_in, bf16[256,1024]{1,0:T(8,128)(2,1)} %get-tuple-element.8.gc_in), custom_call_target="tpu_custom_call" | custom-call | tf_op jit(solution)/shard_map/hand_over/pallas_call | solution.py:898
